TPU v7x, 32 devices: a whole 2x2x4 slice. The times are simulated.
32 devices in a mesh: dp: 8 (over z, core), expert: 4 (over y, x).
Axes of the slice: x: 2, y: 2, z: 4, core: 2. Of those that a mesh axis runs over, the one named last changes fastest.
Arguments:
- tokens: bfloat16 [1280, 4096], P('expert', 'dp'), may hold values from -6 to 6
- out_grad: bfloat16 [1280, 4096], P('expert', 'dp'), may hold values from -0.29882812 to 0.29882812
- slot_tokens: int32 [1, 40], replicated, may hold values from 0 to 1279, as said below
- slot_gate: float32 [1, 40], replicated, may hold values from 0.1 to 1
- w_gate: bfloat16 [4, 4096, 2048], P('expert', 'dp'), may hold values from -0.09375 to 0.09375
- w_up: bfloat16 [4, 4096, 2048], P('expert', 'dp'), may hold values from -0.09375 to 0.09375
- w_down: bfloat16 [4, 2048, 4096], P('expert', None, 'dp'), may hold values from -0.0625 to 0.0625
Outputs:
- grad_tokens: bfloat16 [1280, 4096], P('expert', 'dp')
- grad_w_gate: bfloat16 [4, 4096, 2048], P('expert', 'dp')
- grad_w_up: bfloat16 [4, 4096, 2048], P('expert', 'dp')
- grad_w_down: bfloat16 [4, 2048, 4096], P('expert', None, 'dp')
- grad_gates: float32 [4, 10], P('expert')
Inputs may be any that keep to these rules, and one draw needn't show every extreme that they name: `slot_tokens`: row e lists 40 distinct token numbers, ordered by their owner t // 320 ascending. At most 20 of a row come from the 320 tokens of one owner, and in every row exactly 20 come from one owner.
All inputs are finite; a program needn't handle non-finite values.
Results may differ from a plain program's by a relative error of at most 0.0057.
Values may be sent and summed in bfloat16 or wider, within the bound.
A program may use at most 64 MiB of HBM per device.

v0:
```python
import jax
import jax.numpy as jnp
from jax import lax
from jax.sharding import PartitionSpec as P

GROUP = 4


def partner(value, axis, distance):
    mask = 2**distance
    pairs = [(source, source ^ mask) for source in range(lax.axis_size(axis))]
    return lax.ppermute(value, axis, pairs)


def contract_rows(left, right):
    return lax.dot_general(
        left, right, (((0,), (0,)), ((), ())), preferred_element_type=jnp.float32
    )


def contract_cols(left, right):
    return lax.dot_general(
        left, right, (((1,), (1,)), ((), ())), preferred_element_type=jnp.float32
    )


def slot_ranking(owners, owner_count):
    owner_range = jnp.arange(owner_count, dtype=jnp.int32)
    onehot = (owners[:, :, None] == owner_range[None, None, :]).astype(jnp.int32)
    before = jnp.cumsum(onehot, axis=1) - onehot
    return jnp.sum(before * onehot, axis=2)


def gated_grads(upstream, pre_gate, pre_up, sigmoid_gate):
    gate_side = (upstream * pre_up * sigmoid_gate * (1.0 + pre_gate * (1.0 - sigmoid_gate))).astype(
        jnp.bfloat16
    )
    up_side = (upstream * pre_gate * sigmoid_gate).astype(jnp.bfloat16)
    return (gate_side, up_side)


def per_device(tokens, out_grad, slot_tokens, slot_gate, w_gate, w_up, w_down):
    owner_count = lax.axis_size("expert")
    position = lax.axis_index("expert")
    token_rows = tokens.shape[0]
    feature_cols = tokens.shape[1]
    flight_count, capacity = slot_tokens.shape
    bucket_size = GROUP * max(1, capacity // (2 * owner_count))
    owners = slot_tokens // token_rows
    slot_rank = slot_ranking(owners, owner_count)
    is_mine = owners == position
    local_index = slot_tokens - position * token_rows
    expert_rows = jnp.broadcast_to(
        jnp.arange(flight_count, dtype=jnp.int32)[:, None], (flight_count, capacity)
    )
    column_index = jnp.where(is_mine, slot_rank, bucket_size)
    send_table = (
        jnp.zeros((flight_count, bucket_size + 1), jnp.int32)
        .at[expert_rows, column_index]
        .set(local_index)[:, :bucket_size]
    )
    filled = (
        jnp.zeros((flight_count, bucket_size + 1), jnp.int32)
        .at[expert_rows, column_index]
        .set(1)[:, :bucket_size]
    )
    send_index = jnp.repeat(send_table, GROUP, axis=0)
    send_valid = jnp.repeat(filled, GROUP, axis=0) > 0
    input_send = jnp.where(send_valid[:, :, None], tokens[send_index], jnp.zeros((), jnp.bfloat16))
    grad_send = jnp.where(send_valid[:, :, None], out_grad[send_index], jnp.zeros((), jnp.bfloat16))
    input_recv, grad_recv = (
        lax.all_to_all(input_send, "expert", split_axis=0, concat_axis=0, tiled=True),
        lax.all_to_all(grad_send, "expert", split_axis=0, concat_axis=0, tiled=True),
    )
    expert_here = position // GROUP
    quarter = position % GROUP
    owner_here = lax.dynamic_index_in_dim(owners, expert_here, 0, keepdims=False)
    rank_here = lax.dynamic_index_in_dim(slot_rank, expert_here, 0, keepdims=False)
    bucket_flat = owner_here * bucket_size + rank_here
    slot_inputs = input_recv.reshape(owner_count * bucket_size, feature_cols)[bucket_flat]
    slot_grads = grad_recv.reshape(owner_count * bucket_size, feature_cols)[bucket_flat]
    gates_here = lax.dynamic_index_in_dim(slot_gate, expert_here, 0, keepdims=False)
    gate_weight = w_gate[0]
    up_weight = w_up[0]
    down_weight = w_down[0]
    part_gate = jnp.dot(slot_inputs, gate_weight, preferred_element_type=jnp.float32)
    part_up = jnp.dot(slot_inputs, up_weight, preferred_element_type=jnp.float32)
    pre_gate, pre_up = lax.psum((part_gate, part_up), "dp")
    sigmoid_gate = jax.nn.sigmoid(pre_gate)
    hidden = (pre_gate * sigmoid_gate * pre_up).astype(jnp.bfloat16)
    local_out = jnp.dot(hidden, down_weight, preferred_element_type=jnp.float32)
    gate_part = jnp.sum(slot_grads.astype(jnp.float32) * local_out, axis=1)
    scaled = (gates_here[:, None] * slot_grads.astype(jnp.float32)).astype(jnp.bfloat16)
    grad_down = contract_rows(hidden, scaled).astype(jnp.bfloat16)
    part_hidden = contract_cols(scaled, down_weight)
    grad_hidden = lax.psum(part_hidden, "dp")
    gate_side, up_side = gated_grads(grad_hidden, pre_gate, pre_up, sigmoid_gate)
    gate_total = lax.psum(gate_part, "dp")
    grad_gate_weight = contract_rows(slot_inputs, gate_side).astype(jnp.bfloat16)
    grad_up_weight = contract_rows(slot_inputs, up_side).astype(jnp.bfloat16)
    slot_back = contract_cols(gate_side, gate_weight) + contract_cols(up_side, up_weight)
    for bit_number in range(GROUP.bit_length() - 1):
        gate_total = gate_total + partner(gate_total, "expert", bit_number)
    outgoing = (
        jnp.zeros((owner_count * bucket_size, feature_cols), jnp.float32)
        .at[bucket_flat]
        .set(slot_back)
    )
    incoming = lax.all_to_all(
        outgoing.reshape(owner_count, bucket_size, feature_cols),
        "expert",
        split_axis=0,
        concat_axis=0,
        tiled=True,
    )
    target = jnp.where(send_valid, send_index, token_rows)
    summed = (
        jnp.zeros((token_rows + 1, feature_cols), jnp.float32)
        .at[target.reshape(-1)]
        .add(incoming.reshape(-1, feature_cols))
    )
    grad_tokens = summed[:token_rows].astype(jnp.bfloat16)
    gate_width = capacity // GROUP
    grad_gates = lax.dynamic_slice_in_dim(gate_total, quarter * gate_width, gate_width)[None, :]
    return (grad_tokens, grad_gate_weight[None], grad_up_weight[None], grad_down[None], grad_gates)


def solution(mesh):
    in_specs = (
        P("expert", "dp"),
        P("expert", "dp"),
        P(),
        P(),
        P("expert", "dp", None),
        P("expert", "dp", None),
        P("expert", None, "dp"),
    )
    out_specs = (
        P("expert", "dp"),
        P("expert", "dp", None),
        P("expert", "dp", None),
        P("expert", None, "dp"),
        P("expert", None),
    )
    return jax.shard_map(
        per_device, mesh=mesh, in_specs=in_specs, out_specs=out_specs, check_vma=False
    )
```

profile of v0, /device:TPU:0, one launch (start us, length us, event | category | flops | bytes accessed | tf_op | source)
XLA Modules:
  0.0 139.4 jit_solution(10916364565612315027)
XLA Ops:
  7.2 0.8 subtract_bitcast_fusion
  9.9 1.8 %gather_fusion.2 = bf16[80,512]{1,0:T(8,128)(2,1)S(1)} fusion(bf16[320,512]{1,0:T(8,128)(2,1)} %param.7, s32[1024]{0:T(1024)S(1)} %pad_clamp_fusion.1), kind=kCustom, calls=%fused_computation.2 | custom fusion | bytes 164160 | tf_op jit(solution)/shard_map/gather | solution.py:69
  11.7 1.8 %gather_fusion = bf16[80,512]{1,0:T(8,128)(2,1)S(1)} fusion(bf16[320,512]{1,0:T(8,128)(2,1)} %param.8, s32[1024]{0:T(1024)S(1)} %pad_clamp_fusion.1), kind=kCustom, calls=%fused_computation | custom fusion | bytes 164160 | tf_op jit(solution)/shard_map/gather | solution.py:70
  13.5 0.8 broadcast_select_fusion.1
  14.3 5.2 %all-to-all-start = ((bf16[4,20,512]{2,1,0:T(8,128)(2,1)}), bf16[4,20,512]{2,1,0:T(8,128)(2,1)S(1)}, u32[]{:S(2)}, u32[]{:S(2)}) async-start(bf16[4,20,512]{2,1,0:T(8,128)(2,1)} %get-tuple-element.11), calls=%async_computation | async-start | bytes 196608 | tf_op jit(solution)/shard_map/all_to_all | solution.py:73
  19.5 4.9 %all-to-all-done = bf16[4,20,512]{2,1,0:T(8,128)(2,1)S(1)} async-done(((bf16[4,20,512]{2,1,0:T(8,128)(2,1)}), bf16[4,20,512]{2,1,0:T(8,128)(2,1)S(1)}, u32[]{:S(2)}, u32[]{:S(2)}) %all-to-all-start) | async-done | bytes 81952 | tf_op jit(solution)/shard_map/all_to_all | solution.py:73
  24.4 3.3 %all-to-all-start.1 = ((bf16[4,20,512]{2,1,0:T(8,128)(2,1)}), bf16[4,20,512]{2,1,0:T(8,128)(2,1)S(1)}, u32[]{:S(2)}, u32[]{:S(2)}) async-start(bf16[4,20,512]{2,1,0:T(8,128)(2,1)} %get-tuple-element.12), calls=%async_computation.1 | async-start | bytes 196608 | tf_op jit(solution)/shard_map/all_to_all | solution.py:72
  28.4 4.2 %all-to-all-done.1 = bf16[4,20,512]{2,1,0:T(8,128)(2,1)S(1)} async-done(((bf16[4,20,512]{2,1,0:T(8,128)(2,1)}), bf16[4,20,512]{2,1,0:T(8,128)(2,1)S(1)}, u32[]{:S(2)}, u32[]{:S(2)}) %all-to-all-start.1) | async-done | bytes 81952 | tf_op jit(solution)/shard_map/all_to_all | solution.py:72
  33.3 1.2 fusion.5
  35.0 1.2 fusion.9
  36.2 1.5 %fusion.13 = f32[40,2048]{1,0:T(8,128)} fusion(bf16[1,2048,512]{2,1,0:T(8,128)(2,1)S(1)} %copy-done.3, bf16[40,512]{1,0:T(8,128)(2,1)S(1)} %gather_fusion.1, f32[40]{0:T(128)S(1)} %bitcast.80), kind=kOutput, calls=%fused_computation.24 | convolution fusion | flops 83947520 | bytes 2465952 | tf_op jit(solution)/shard_map/dot_general | solution.py:22
  37.8 58.4 %all-reduce.4.cloned.1.call-done = (f32[40,2048]{1,0:T(8,128)}, f32[40,2048]{1,0:T(8,128)}, f32[40,2048]{1,0:T(8,128)}) async-done(((f32[40,2048]{1,0:T(8,128)}, f32[40,2048]{1,0:T(8,128)}, f32[40,2048]{1,0:T(8,128)}), (f32[40,2048]{1,0:T(8,128)}, f32[40,2048]{1,0:T(8,128)}, f32[40,2048]{1,0:T(8,128)})) %all-reduce.4.cloned.1.call-update) | async-done | bytes 983056 | tf_op jit(solution)/shard_map/psum | solution.py:88
  96.2 1.3 multiply_convert_fusion
  97.6 2.2 %fusion.21 = f32[40]{0:T(128)S(1)} fusion(bf16[40,2048]{1,0:T(8,128)(2,1)S(1)} %get-tuple-element.8, bf16[1,2048,512]{2,1,0:T(8,128)(2,1)} %param.13, bf16[40,512]{1,0:T(8,128)(2,1)S(1)} %gather_fusion.1), kind=kOutput, calls=%fused_computation.28 | convolution fusion | flops 83947480 | bytes 2302112 | tf_op jit(solution)/shard_map/dot_general | solution.py:91
  99.8 2.1 %fusion.2 = bf16[1,2048,512]{2,1,0:T(8,128)(2,1)} fusion(bf16[40,2048]{1,0:T(8,128)(2,1)S(1)} %get-tuple-element.8, bf16[40,512]{1,0:T(8,128)(2,1)S(1)} %gather_fusion.1, f32[40]{0:T(128)S(1)} %bitcast.81), kind=kOutput, calls=%fused_computation.13 | convolution fusion | flops 84996096 | bytes 2302112 | tf_op jit(solution)/shard_map/dot_general | solution.py:16
  101.9 13.6 %psum.31 = f32[40]{0:T(128)S(1)} all-reduce(f32[40]{0:T(128)S(1)} %fusion.21), channel_id=1, replica_groups=mesh['dp'=8,'expert'=4] {'dp'}, use_global_device_ids=true, to_apply=%region_10.11 | all-reduce | flops 40 | bytes 320 | tf_op jit(solution)/shard_map/psum | solution.py:98
  115.4 1.5 %collective-permute-start = (f32[40]{0:T(128)S(1)}, f32[40]{0:T(128)S(1)}, u32[]{:S(2)}, u32[]{:S(2)}) collective-permute-start(f32[40]{0:T(128)S(1)} %psum.31), channel_id=1, source_target_pairs={{0,1},{1,0},{2,3},{3,2},{4,5},{5,4},{6,7},{7,6},{8,9},{9,8},{10,11... | collective-permute-start | bytes 488 | tf_op jit(solution)/shard_map/ppermute | solution.py:12
  117.7 2.0 %fusion.1 = bf16[1,512,2048]{2,1,0:T(8,128)(2,1)} fusion(bf16[40,512]{1,0:T(8,128)(2,1)S(1)} %gather_fusion.3, bf16[40,2048]{1,0:T(8,128)(2,1)S(1)} %get-tuple-element.10), kind=kOutput, calls=%fused_computation.12 | convolution fusion | flops 84934656 | bytes 2301952 | tf_op jit(solution)/shard_map/dot_general | solution.py:16
  120.5 0.8 scatter_custom_fusion.2
  122.0 3.4 %all-to-all-start.2 = ((f32[4,20,512]{2,1,0:T(8,128)}), f32[4,20,512]{2,1,0:T(8,128)S(1)}, u32[]{:S(2)}, u32[]{:S(2)}) async-start(f32[4,20,512]{2,1,0:T(8,128)} %reshape.273), calls=%async_computation.2 | async-start | bytes 393216 | tf_op jit(solution)/shard_map/all_to_all | solution.py:109
  125.4 2.0 %collective-permute-start.1 = (f32[40]{0:T(128)S(1)}, f32[40]{0:T(128)S(1)}, u32[]{:S(2)}, u32[]{:S(2)}) collective-permute-start(f32[40]{0:T(128)S(1)} %add.94), channel_id=1, source_target_pairs={{0,2},{1,3},{2,0},{3,1},{4,6},{5,7},{6,4},{7,5},{8,10},{9,11},{10,... | collective-permute-start | bytes 488 | tf_op jit(solution)/shard_map/ppermute | solution.py:12
  127.3 2.1 %fusion = bf16[1,512,2048]{2,1,0:T(8,128)(2,1)} fusion(bf16[40,512]{1,0:T(8,128)(2,1)S(1)} %gather_fusion.3, bf16[40,2048]{1,0:T(8,128)(2,1)S(1)} %get-tuple-element.9), kind=kOutput, calls=%fused_computation.11 | convolution fusion | flops 84934656 | bytes 2301952 | tf_op jit(solution)/shard_map/dot_general | solution.py:16
  130.5 1.2 scatter_custom_fusion.3
  131.8 0.8 slice.38
  (49 shorter events, 7.2 us)
Async XLA Ops:
  7.2 26.1 %copy-start = (bf16[1,512,2048]{2,1,0:T(8,128)(2,1)S(1)}, bf16[1,512,2048]{2,1,0:T(8,128)(2,1)}, u32[]{:S(2)}) copy-start(bf16[1,512,2048]{2,1,0:T(8,128)(2,1)} %param.11) | copy-start | bytes 6291460
  14.3 10.1 %all-to-all-start = ((bf16[4,20,512]{2,1,0:T(8,128)(2,1)}), bf16[4,20,512]{2,1,0:T(8,128)(2,1)S(1)}, u32[]{:S(2)}, u32[]{:S(2)}) async-start(bf16[4,20,512]{2,1,0:T(8,128)(2,1)} %get-tuple-element.11), calls=%async_computation | async-start | bytes 196608 | tf_op jit(solution)/shard_map/all_to_all | solution.py:73
  24.4 8.2 %all-to-all-start.1 = ((bf16[4,20,512]{2,1,0:T(8,128)(2,1)}), bf16[4,20,512]{2,1,0:T(8,128)(2,1)S(1)}, u32[]{:S(2)}, u32[]{:S(2)}) async-start(bf16[4,20,512]{2,1,0:T(8,128)(2,1)} %get-tuple-element.12), calls=%async_computation.1 | async-start | bytes 196608 | tf_op jit(solution)/shard_map/all_to_all | solution.py:72
  27.7 68.5 %all-reduce.4.cloned.1.call-start = ((), (), s32[]{:S(2)}) async-start(), calls=%async_computation.3 | async-start | bytes 1966080 | tf_op jit(solution)/shard_map/psum | solution.py:88
  33.3 1.7 %copy-start.1 = (bf16[1,512,2048]{2,1,0:T(8,128)(2,1)S(1)}, bf16[1,512,2048]{2,1,0:T(8,128)(2,1)}, u32[]{:S(2)}) copy-start(bf16[1,512,2048]{2,1,0:T(8,128)(2,1)} %param.12) | copy-start | bytes 6291460
  33.3 2.9 %copy-start.3 = (bf16[1,2048,512]{2,1,0:T(8,128)(2,1)S(1)}, bf16[1,2048,512]{2,1,0:T(8,128)(2,1)}, u32[]{:S(2)}) copy-start(bf16[1,2048,512]{2,1,0:T(8,128)(2,1)} %param.13) | copy-start | bytes 6291460
  33.3 2.9 %copy-start.4 = (f32[1,40]{1,0:T(1,128)S(1)}, f32[1,40]{1,0:T(1,128)}, u32[]{:S(2)}) copy-start(f32[1,40]{1,0:T(1,128)} %param.10) | copy-start | bytes 484
  115.4 9.9 %collective-permute-start = (f32[40]{0:T(128)S(1)}, f32[40]{0:T(128)S(1)}, u32[]{:S(2)}, u32[]{:S(2)}) collective-permute-start(f32[40]{0:T(128)S(1)} %psum.31), channel_id=1, source_target_pairs={{0,1},{1,0},{2,3},{3,2},{4,5},{5,4},{6,7},{7,6},{8,9},{9,8},{10,11... | collective-permute-start | bytes 488 | tf_op jit(solution)/shard_map/ppermute | solution.py:12
  116.9 2.8 %copy-start.2 = (bf16[1,512,2048]{2,1,0:T(8,128)(2,1)S(1)}, bf16[1,512,2048]{2,1,0:T(8,128)(2,1)}, u32[]{:S(2)}) copy-start(bf16[1,512,2048]{2,1,0:T(8,128)(2,1)} %param.12) | copy-start | bytes 6291460
  122.0 8.5 %all-to-all-start.2 = ((f32[4,20,512]{2,1,0:T(8,128)}), f32[4,20,512]{2,1,0:T(8,128)S(1)}, u32[]{:S(2)}, u32[]{:S(2)}) async-start(f32[4,20,512]{2,1,0:T(8,128)} %reshape.273), calls=%async_computation.2 | async-start | bytes 393216 | tf_op jit(solution)/shard_map/all_to_all | solution.py:109
  125.4 4.4 %collective-permute-start.1 = (f32[40]{0:T(128)S(1)}, f32[40]{0:T(128)S(1)}, u32[]{:S(2)}, u32[]{:S(2)}) collective-permute-start(f32[40]{0:T(128)S(1)} %add.94), channel_id=1, source_target_pairs={{0,2},{1,3},{2,0},{3,1},{4,6},{5,7},{6,4},{7,5},{8,10},{9,11},{10,... | collective-permute-start | bytes 488 | tf_op jit(solution)/shard_map/ppermute | solution.py:12
Sparse Core Ops, SparseCore 0:
  37.8 58.3 all-reduce.3
where the time goes:
time: 140 us; the launch traced here: 139 us
  waiting for transfers between devices  68.1 us (49%)
  starting transfers between devices  15.4 us (11%)
  between operations  14.3 us (10%)
  matrix products  13.7 us (10%)
  blocking collectives  13.6 us (10%)
  local copies, waits for them, and re-layouts  9.83 us (7%)
  other arithmetic  4.55 us (3%)
    psum x1, waiting for transfers between devices, per_device(): pre_gate, pre_up = lax.psum((part_gate, part_up), 'dp')  58.4 us
    psum x1, blocking collectives, per_device(): gate_total = lax.psum(gate_part, 'dp')  13.6 us
    dot_general x3, matrix products, contract_rows(): lax.dot_general(left, right, (((0,), (0,)), ((), ())), preferred_element_...  6.19 us
    all_to_all x1, starting transfers between devices, per_device(): lax.all_to_all(grad_send, 'expert', split_axis=0, concat_axis=0, tiled=True)  5.16 us
    all_to_all x1, waiting for transfers between devices, per_device(): lax.all_to_all(grad_send, 'expert', split_axis=0, concat_axis=0, tiled=True)  4.93 us
    all_to_all x1, waiting for transfers between devices, per_device(): lax.all_to_all(input_send, 'expert', split_axis=0, concat_axis=0, tiled=T...  4.16 us
    ppermute x2, starting transfers between devices, partner(): return lax.ppermute(value, axis, pairs)  3.48 us
    all_to_all x1, starting transfers between devices, per_device(): lax.all_to_all(outgoing.reshape(owner_count, bucket_size, feature_cols),...  3.37 us
  transfers between devices with their start and end apart: 6, of which 5 were waited for; matrix products, arithmetic and copies ran while one was open for 6% of the time, Pallas kernels for 0%

commit v1 on v0

v1 whole, which is shorter than its diff:
```python
import functools

import jax
import jax.numpy as jnp
from jax import lax
from jax.experimental import pallas as pl
from jax.experimental.pallas import tpu as pltpu
from jax.sharding import PartitionSpec as P

GROUP = 4
MESH = pl.DeviceIdType.MESH
BF16 = jnp.bfloat16
F32 = jnp.float32


def ceil_to(value, step):
    return -(-value // step) * step


def mm(left, right, left_dim, right_dim):
    return lax.dot_general(
        left, right, (((left_dim,), (right_dim,)), ((), ())), preferred_element_type=F32
    )


def iota(shape, dim):
    return lax.broadcasted_iota(jnp.int32, shape, dim)


def count_below(row, bound):
    return jnp.sum(jnp.where(row < bound, 1.0, 0.0), axis=1, keepdims=True).astype(jnp.int32)


def rank_mask(row, low, high, rows, columns_dim):
    capacity = row.shape[1]
    start, end = count_below(row, low), count_below(row, high)
    shape = (rows, capacity) if columns_dim == 1 else (capacity, rows)
    slot, rank = iota(shape, columns_dim), iota(shape, 1 - columns_dim)
    return (slot == rank + start) & (slot < end)


def local_index(row, low, high, rows):
    mask = rank_mask(row, low, high, rows, 1)
    shifted = (row + (1 - low)).astype(F32)
    picked = jnp.sum(jnp.where(mask, shifted, 0.0), axis=1, keepdims=True)
    return picked.astype(jnp.int32) - 1


def row_to_column(row):
    size = row.shape[1]
    eye = iota((size, size), 0) == iota((size, size), 1)
    return jnp.sum(jnp.where(eye, row, 0.0), axis=1, keepdims=True)


def split_two(value):
    high = value.astype(BF16).astype(F32)
    return [high, value - high]


def pick_row(table, index):
    if table.shape[0] == 1:
        return table
    return jnp.sum(jnp.where(iota(table.shape, 0) == index, table, 0.0), axis=0, keepdims=True)


def pad_rows(value, rows):
    if value.shape[0] == rows:
        return value
    return jnp.concatenate([value, jnp.zeros((rows - value.shape[0], value.shape[1]), value.dtype)], axis=0)


def exchange_kernel(
    cfg,
    slot_hbm,
    gate_hbm,
    tokens_hbm,
    grad_hbm,
    wg_hbm,
    wu_hbm,
    wd_hbm,
    gwg_ref,
    gwu_ref,
    gwd_ref,
    ret_ref,
    gsum_ref,
    where_ref,
    slot_ref,
    gate_ref,
    tokens,
    out_grad,
    wg,
    wu,
    wd,
    pick_send,
    pick_recv,
    pair_send_a,
    pair_send_b,
    pair_recv_a,
    pair_recv_b,
    z_own_a,
    z_own_b,
    z_send_a,
    z_send_b,
    z_recv_a,
    z_recv_b,
    hid_blocks,
    side_blocks,
    part_blocks,
    back_send,
    back_recv,
    local_sem,
    pick_ssem,
    pick_rsem,
    pair_ssem,
    pair_rsem,
    z_ssem,
    z_rsem,
    ag_ssem,
    fwd_ssem,
    ag_rsem,
    part_ssem,
    part_rsem,
    back_ssem,
    back_rsem,
):
    nx, nz, cap, flight, rb = cfg.nx, cfg.nz, cfg.cap, cfg.flight, cfg.rb
    half, width, fc, tok = cfg.half, cfg.width, cfg.fc, cfg.tok
    nd = 2 * nz
    me_x = lax.axis_index("expert")
    me_d = lax.axis_index("dp")
    my_z, my_c = me_d // 2, lax.rem(me_d, 2)
    other_c = 1 - my_c
    partner = my_z * 2 + other_c
    expert_here = me_x // GROUP

    x_peers = [lax.rem(me_x + k, nx) for k in range(1, nx)]
    z_peers = [lax.rem(my_z + k, nz) for k in range(1, nz)]
    d_peers = [lax.rem(me_d + k, nd) for k in range(1, nd)]
    barrier = pltpu.get_barrier_semaphore()
    for peer in x_peers:
        pl.semaphore_signal(barrier, inc=1, device_id=(me_d, peer), device_id_type=MESH)
    for peer in d_peers:
        pl.semaphore_signal(barrier, inc=1, device_id=(peer, me_x), device_id_type=MESH)

    pairs = (
        (slot_hbm, slot_ref),
        (gate_hbm, gate_ref),
        (tokens_hbm, tokens),
        (grad_hbm, out_grad),
        (wg_hbm.at[0], wg),
        (wu_hbm.at[0], wu),
        (wd_hbm.at[0], wd),
    )
    loads = [pltpu.make_async_copy(src, dst, local_sem.at[i]) for i, (src, dst) in enumerate(pairs)]
    for load in loads:
        load.start()

    def remote(src, dst, send_sem, recv_sem, target):
        return pltpu.make_async_remote_copy(
            src_ref=src,
            dst_ref=dst,
            send_sem=send_sem,
            recv_sem=recv_sem,
            device_id=target,
            device_id_type=MESH,
        )

    sends = []

    def launch(copy):
        copy.start()
        sends.append(copy)

    loads[0].wait()
    loads[1].wait()
    slots = slot_ref[...]
    picks = []
    for e in range(flight):
        where = local_index(slots[e : e + 1], me_x * tok, (me_x + 1) * tok, rb)
        where_ref[e] = where
        picks.append((where == iota((rb, tok), 1)).astype(F32).astype(BF16))
    loads[2].wait()
    loads[3].wait()
    for e in range(flight):
        rows = [mm(picks[e], tokens[...], 1, 0), mm(picks[e], out_grad[...], 1, 0)]
        pick_send[e] = jnp.concatenate(rows, axis=0).astype(BF16)
    pick_recv[me_x] = pick_send[expert_here]
    pl.semaphore_wait(barrier, len(x_peers) + len(d_peers))

    def pick_copy(k, peer, slot):
        return remote(
            pick_send.at[peer // GROUP], pick_recv.at[slot], pick_ssem.at[k], pick_rsem.at[slot], (me_d, peer)
        )

    for k, peer in enumerate(x_peers):
        launch(pick_copy(k, peer, me_x))

    slot_row = pick_row(slots.astype(F32), expert_here).astype(jnp.int32)
    gate_col = row_to_column(pick_row(gate_ref[...], expert_here))
    place_x, place_g = [], []
    empty = jnp.zeros((cap, rb), F32)
    for o in range(nx):
        mask = rank_mask(slot_row, o * tok, (o + 1) * tok, rb, 0).astype(F32)
        place_x += [mask, empty]
        place_g += [empty, mask]
    place = jnp.concatenate(
        [jnp.concatenate(place_x, axis=1), jnp.concatenate(place_g, axis=1)], axis=0
    ).astype(BF16)
    for k, peer in enumerate(x_peers):
        pick_copy(k, peer, peer).wait_recv()
    both = mm(place, pick_recv[...].reshape(nx * 2 * rb, fc), 1, 0)
    x = both[:cap].astype(BF16)
    scaled = (gate_col * both[cap:]).astype(BF16)
    grads = both[cap:].astype(BF16)

    def first_pair(core):
        cols = pl.ds(pl.multiple_of(core * half, half), half)
        return jnp.concatenate([mm(x, wg[:, cols], 1, 0), mm(x, wu[:, cols], 1, 0)], axis=0)

    def hidden_part(core):
        cols = pl.ds(pl.multiple_of(core * half, half), half)
        return mm(grads, wd[cols, :], 1, 1)

    def pair_copy(i):
        src, dst = ((pair_send_a, pair_recv_a), (pair_send_b, pair_recv_b))[i]
        return remote(src, dst, pair_ssem.at[i], pair_rsem.at[i], (partner, me_x))

    def z_copy(i, k, peer, slot):
        src, dst = ((z_send_a, z_recv_a), (z_send_b, z_recv_b))[i]
        return remote(
            src.at[peer], dst.at[slot], z_ssem.at[i, k], z_rsem.at[i, slot], (peer * 2 + my_c, me_x)
        )

    def z_start(i, own):
        got = (pair_recv_a, pair_recv_b)[i]
        send = (z_send_a, z_send_b)[i]
        keep = (z_own_a, z_own_b)[i]
        pair_copy(i).wait_recv()
        for j in range(nz):
            cols = slice(j * width, (j + 1) * width)
            total = own[:, cols] + got[:, cols]
            keep[j] = total
            send[j] = pad_rows(total, send.shape[1]).astype(BF16)
        for k, peer in enumerate(z_peers):
            launch(z_copy(i, k, peer, my_z))

    def z_finish(i):
        recv = (z_recv_a, z_recv_b)[i]
        total = (z_own_a, z_own_b)[i][my_z]
        for k, peer in enumerate(z_peers):
            z_copy(i, k, peer, peer).wait_recv()
            total = total + recv[peer].astype(F32)[: total.shape[0]]
        return total

    loads[4].wait()
    loads[5].wait()
    pair_send_a[...] = first_pair(other_c)
    launch(pair_copy(0))
    own_a = first_pair(my_c)
    z_start(0, own_a)
    loads[6].wait()
    pair_send_b[...] = hidden_part(other_c)
    launch(pair_copy(1))
    own_b = hidden_part(my_c)
    z_start(1, own_b)

    def ag_copy(i, owner, send_sem, target):
        block = (hid_blocks, side_blocks)[i].at[owner]
        return remote(block, block, send_sem, ag_rsem.at[i, owner], (target, me_x))

    def ag_start(i):
        for k, peer in enumerate(z_peers):
            launch(ag_copy(i, me_d, ag_ssem.at[i, k], peer * 2 + my_c))
        launch(ag_copy(i, me_d, fwd_ssem.at[i, 0], partner))

    def ag_forward(i):
        for k, peer in enumerate(z_peers):
            owner = peer * 2 + my_c
            ag_copy(i, owner, ag_ssem.at[i, k], owner).wait_recv()
            launch(ag_copy(i, owner, fwd_ssem.at[i, k + 1], partner))

    def ag_finish(i):
        for k, peer in enumerate([my_z] + z_peers):
            ag_copy(i, peer * 2 + other_c, fwd_ssem.at[i, k], partner).wait_recv()

    total = z_finish(0)
    pre_gate, pre_up = total[:cap], total[cap:]
    sig = 1.0 / (1.0 + jnp.exp(-pre_gate))
    silu = pre_gate * sig
    hidden = silu * pre_up
    hid_blocks[me_d] = pad_rows(hidden, cfg.rows_b).astype(BF16)
    ag_start(0)
    gate_slope = pre_up * sig * (1.0 + pre_gate * (1.0 - sig))
    upstream = z_finish(1)
    grad_hidden = gate_col * upstream
    side_blocks[me_d] = pad_rows(
        jnp.concatenate([grad_hidden * gate_slope, grad_hidden * silu], axis=0), cfg.rows_a
    ).astype(BF16)
    ag_start(1)
    gate_part = jnp.sum(hidden * upstream, axis=1, keepdims=True)
    lines = []
    for k in range(cfg.gate_rows):
        here = iota((cap, width), 0) == iota((cap, width), 1) + k * width
        lines.append(jnp.sum(jnp.where(here, gate_part, 0.0), axis=0, keepdims=True))
    part_blocks[me_d] = pad_rows(jnp.concatenate(lines, axis=0), cfg.part_rows)

    def part_copy(k, peer, slot):
        return remote(part_blocks.at[me_d], part_blocks.at[slot], part_ssem.at[k], part_rsem.at[slot], (peer, me_x))

    for k, peer in enumerate(d_peers):
        launch(part_copy(k, peer, me_d))

    ag_forward(0)

    def gather(blocks, core, start):
        parts = [blocks[j * 2 + core].astype(F32)[start : start + cap] for j in range(nz)]
        return jnp.concatenate(parts, axis=1).astype(BF16)

    def down_grad(core):
        rows = pl.ds(pl.multiple_of(core * half, half), half)
        gwd_ref[0, rows, :] = mm(gather(hid_blocks, core, 0), scaled, 0, 0).astype(BF16)

    down_grad(my_c)
    ag_forward(1)

    def back_half(core):
        cols = pl.ds(pl.multiple_of(core * half, half), half)
        gate_side, up_side = gather(side_blocks, core, 0), gather(side_blocks, core, cap)
        return gate_side, up_side, mm(gate_side, wg[:, cols], 1, 1) + mm(up_side, wu[:, cols], 1, 1)

    mine = back_half(my_c)
    ag_finish(0)
    ag_finish(1)
    others = back_half(other_c)
    back = (mine[2] + others[2]).astype(BF16)

    for k, peer in enumerate(d_peers):
        part_copy(k, peer, peer).wait_recv()
    gates_sum = sum(part_blocks[d] for d in range(nd))
    gate_lines = []
    for k in range(cfg.gate_rows):
        gate_lines += split_two(gates_sum[k : k + 1])
    lines = pad_rows(jnp.concatenate(gate_lines, axis=0), cfg.back_rows - rb)
    if width < fc:
        lines = jnp.concatenate([lines, jnp.zeros((lines.shape[0], fc - width), F32)], axis=1)
    for o in range(nx):
        mask = rank_mask(slot_row, o * tok, (o + 1) * tok, rb, 1).astype(F32).astype(BF16)
        back_send[o] = jnp.concatenate([mm(mask, back, 1, 0), lines], axis=0).astype(BF16)
    back_recv[me_x] = back_send[me_x]

    def back_copy(k, peer, slot):
        return remote(
            back_send.at[peer], back_recv.at[slot], back_ssem.at[k], back_rsem.at[slot], (me_d, peer)
        )

    for k, peer in enumerate(x_peers):
        launch(back_copy(k, peer, me_x))

    down_grad(other_c)
    for core, (gate_side, up_side, _) in ((my_c, mine), (other_c, others)):
        cols = pl.ds(pl.multiple_of(core * half, half), half)
        gwg_ref[0, :, cols] = mm(x, gate_side, 0, 0).astype(BF16)
        gwu_ref[0, :, cols] = mm(x, up_side, 0, 0).astype(BF16)
    for k, peer in enumerate(x_peers):
        back_copy(k, peer, peer).wait_recv()
    for e in range(flight):
        ret_ref[e] = sum(back_recv[e * GROUP + q, :rb].astype(F32) for q in range(GROUP))
    gsum_ref[...] = sum(
        back_recv[expert_here * GROUP + q, rb:].astype(F32)[:, :width] for q in range(GROUP)
    )
    for copy in sends:
        copy.wait_send()


def finish_kernel(
    cfg,
    gwg_ref,
    gwu_ref,
    gwd_ref,
    ret_ref,
    gsum_ref,
    where_ref,
    tok_out,
    wg_out,
    wu_out,
    wd_out,
    gates_out,
    tok_vmem,
    sem,
):
    copies = [
        pltpu.make_async_copy(src, dst, sem.at[i])
        for i, (src, dst) in enumerate(((gwg_ref, wg_out), (gwu_ref, wu_out), (gwd_ref, wd_out)))
    ]
    for copy in copies:
        copy.start()
    me_x = lax.axis_index("expert")
    total = None
    for e in range(cfg.flight):
        spread = (where_ref[e] == iota((cfg.rb, cfg.tok), 1)).astype(F32).astype(BF16)
        term = mm(spread, ret_ref[e].astype(BF16), 0, 0)
        total = term if total is None else total + term
    tok_vmem[...] = total.astype(BF16)
    copies.append(pltpu.make_async_copy(tok_vmem, tok_out, sem.at[3]))
    copies[3].start()
    wide = cfg.cap // GROUP
    first = lax.rem(me_x, GROUP) * wide
    gates = jnp.zeros((1, wide), F32)
    for k in range(cfg.gate_rows):
        line = gsum_ref[2 * k : 2 * k + 1, :] + gsum_ref[2 * k + 1 : 2 * k + 2, :]
        shape = (wide, cfg.width)
        here = iota(shape, 1) + k * cfg.width == iota(shape, 0) + first
        column = jnp.sum(jnp.where(here, line, 0.0), axis=1, keepdims=True)
        eye = iota((wide, wide), 0) == iota((wide, wide), 1)
        gates = gates + jnp.sum(jnp.where(eye, column, 0.0), axis=0, keepdims=True)
    gates_out[...] = gates
    for copy in copies:
        copy.wait()


class Sizes:
    pass


def per_device(mesh_shape, tokens, out_grad, slot_tokens, slot_gate, w_gate, w_up, w_down):
    c = Sizes()
    c.nx, nd = mesh_shape["expert"], mesh_shape["dp"]
    c.nz = nd // 2
    c.flight, c.cap = slot_tokens.shape
    c.tok, c.fc = tokens.shape
    ffq = w_gate.shape[2]
    c.half = ffq // 2
    c.width = c.half // c.nz
    most = 20
    c.rb = ceil_to(most, 8)
    c.gate_rows = ceil_to(c.cap, c.width) // c.width
    c.part_rows = ceil_to(c.gate_rows, 8)
    c.rows_a, c.rows_b = ceil_to(2 * c.cap, 16), ceil_to(c.cap, 16)
    c.back_rows = ceil_to(c.rb + 2 * c.gate_rows, 16)
    vmem = pl.BlockSpec(memory_space=pltpu.VMEM)
    hbm = pl.BlockSpec(memory_space=pltpu.HBM)
    dma = pltpu.SemaphoreType.DMA
    shape = jax.ShapeDtypeStruct
    grads = (
        shape((1, c.fc, ffq), BF16),
        shape((1, c.fc, ffq), BF16),
        shape((1, ffq, c.fc), BF16),
    )
    args = [
        pltpu.with_memory_space_constraint(value, pltpu.HBM)
        for value in (slot_tokens, slot_gate, tokens, out_grad, w_gate, w_up, w_down)
    ]
    parts = pl.pallas_call(
        functools.partial(exchange_kernel, c),
        out_shape=grads
        + (
            shape((c.flight, c.rb, c.fc), F32),
            shape((c.back_rows - c.rb, c.width), F32),
            shape((c.flight, c.rb, 1), jnp.int32),
        ),
        in_specs=[hbm] * 7,
        out_specs=[vmem] * 6,
        scratch_shapes=[
            pltpu.VMEM(slot_tokens.shape, jnp.int32),
            pltpu.VMEM(slot_gate.shape, F32),
            pltpu.VMEM((c.tok, c.fc), BF16),
            pltpu.VMEM((c.tok, c.fc), BF16),
            pltpu.VMEM((c.fc, ffq), BF16),
            pltpu.VMEM((c.fc, ffq), BF16),
            pltpu.VMEM((ffq, c.fc), BF16),
            pltpu.VMEM((c.flight, 2 * c.rb, c.fc), BF16),
            pltpu.VMEM((c.nx, 2 * c.rb, c.fc), BF16),
            pltpu.VMEM((2 * c.cap, c.half), F32),
            pltpu.VMEM((c.cap, c.half), F32),
            pltpu.VMEM((2 * c.cap, c.half), F32),
            pltpu.VMEM((c.cap, c.half), F32),
            pltpu.VMEM((c.nz, 2 * c.cap, c.width), F32),
            pltpu.VMEM((c.nz, c.cap, c.width), F32),
            pltpu.VMEM((c.nz, c.rows_a, c.width), BF16),
            pltpu.VMEM((c.nz, c.rows_b, c.width), BF16),
            pltpu.VMEM((c.nz, c.rows_a, c.width), BF16),
            pltpu.VMEM((c.nz, c.rows_b, c.width), BF16),
            pltpu.VMEM((nd, c.rows_b, c.width), BF16),
            pltpu.VMEM((nd, c.rows_a, c.width), BF16),
            pltpu.VMEM((nd, c.part_rows, c.width), F32),
            pltpu.VMEM((c.nx, c.back_rows, c.fc), BF16),
            pltpu.VMEM((c.nx, c.back_rows, c.fc), BF16),
            dma((7,)),
            dma((c.nx,)),
            dma((c.nx,)),
            dma((2,)),
            dma((2,)),
            dma((2, c.nz)),
            dma((2, c.nz)),
            dma((2, c.nz)),
            dma((2, c.nz)),
            dma((2, nd)),
            dma((nd,)),
            dma((nd,)),
            dma((c.nx,)),
            dma((c.nx,)),
        ],
        compiler_params=pltpu.CompilerParams(
            collective_id=0, has_side_effects=True, vmem_limit_bytes=40 * 1024 * 1024
        ),
        name="exchange",
    )(*args)

    return pl.pallas_call(
        functools.partial(finish_kernel, c),
        out_shape=(shape((c.tok, c.fc), BF16),) + grads + (shape((1, c.cap // GROUP), F32),),
        in_specs=[vmem] * 6,
        out_specs=[hbm] * 4 + [vmem],
        scratch_shapes=[pltpu.VMEM((c.tok, c.fc), BF16), dma((4,))],
        compiler_params=pltpu.CompilerParams(vmem_limit_bytes=40 * 1024 * 1024),
        name="finish",
    )(*parts)


def solution(mesh):
    in_specs = (
        P("expert", "dp"),
        P("expert", "dp"),
        P(),
        P(),
        P("expert", "dp", None),
        P("expert", "dp", None),
        P("expert", None, "dp"),
    )
    out_specs = (
        P("expert", "dp"),
        P("expert", "dp", None),
        P("expert", "dp", None),
        P("expert", None, "dp"),
        P("expert", None),
    )
    return jax.shard_map(
        functools.partial(per_device, dict(mesh.shape)),
        mesh=mesh,
        in_specs=in_specs,
        out_specs=out_specs,
        check_vma=False,
    )
```

time: 140 us -> 34.9 us (0.25)
  waiting for transfers between devices: 68.1 us -> 0 us
  Pallas kernels: 0 us -> 34.1 us
  starting transfers between devices: 15.4 us -> 0 us
  matrix products: 13.7 us -> 0 us
  between operations: 14.3 us -> 0.64 us
  blocking collectives: 13.6 us -> 0 us
  local copies, waits for them, and re-layouts: 9.83 us -> 0 us
  other arithmetic: 4.55 us -> 0 us
    psum x1 -> x0, waiting for transfers between devices: 58.4 us -> none  [per_device(): pre_gate, pre_up = lax.psum((part_gate, part_up), 'dp')]
    pallas_call x0 -> x2, Pallas kernels: none -> 34.1 us  [the longest x1 30.8 us: per_device(): pl.pallas_call(functools.partial(exchange_kernel, c), out_shape=grads + (...]
    dot_general x9 -> x0, matrix products: 13.7 us -> none  [the longest x3 6.19 us: contract_rows(): lax.dot_general(left, right, (((0,), (0,)), ((), ())), preferred_element_...]
    psum x1 -> x0, blocking collectives: 13.6 us -> none  [per_device(): gate_total = lax.psum(gate_part, 'dp')]
    all_to_all x3 -> x0, starting transfers between devices: 11.8 us -> none  [the longest x1 5.16 us: per_device(): lax.all_to_all(grad_send, 'expert', split_axis=0, concat_axis=0, tiled=True)]
    all_to_all x3 -> x0, waiting for transfers between devices: 9.26 us -> none  [the longest x1 4.93 us: per_device(): lax.all_to_all(grad_send, 'expert', split_axis=0, concat_axis=0, tiled=True)]
    gather x6 -> x0, local copies, waits for them, and re-layouts: 4.87 us -> none  [the longest x2 1.79 us: per_device(): out_grad[send_index]]
    ppermute x2 -> x0, starting transfers between devices: 3.48 us -> none  [partner(): return lax.ppermute(value, axis, pairs)]
  transfers between devices with their start and end apart: 6 -> 0, of which waited for: 5 -> 0; matrix products, arithmetic and copies ran while one was open for 6% -> 0% of each run, Pallas kernels for 0% -> 0%
where the time goes in v1:
time: 34.9 us; the launch traced here: 34.7 us
  Pallas kernels  34.1 us (98%)
  between operations  0.64 us (2%)
    pallas_call x1, Pallas kernels, per_device(): pl.pallas_call(functools.partial(exchange_kernel, c), out_shape=grads + (...  30.8 us
    pallas_call x1, Pallas kernels, per_device(): pl.pallas_call(functools.partial(finish_kernel, c), out_shape=(shape((c.t...  3.28 us

profile of v1, /device:TPU:0, one launch (start us, length us, event | category | flops | bytes accessed | tf_op | source)
XLA Modules:
  0.0 34.7 jit_solution(18178054602532732050)
XLA Ops:
  0.6 30.8 %exchange.1 = (bf16[1,512,2048]{2,1,0:T(8,128)(2,1)S(1)}, bf16[1,512,2048]{2,1,0:T(8,128)(2,1)S(1)}, bf16[1,2048,512]{2,1,0:T(8,128)(2,1)S(1)}, f32[1,24,512]{2,...) custom-call(s32[1,40]{1,0:T(1,128)} %slot_hbm.1, f32[1,40]{1,0:T(1,128)} %gate_hbm.1, ...), custom_call_target="tpu_custom_call" | custom-call | tf_op jit(solution)/shard_map/exchange/pallas_call | solution.py:453
  31.4 3.3 %finish.1 = (bf16[320,512]{1,0:T(8,128)(2,1)}, bf16[1,512,2048]{2,1,0:T(8,128)(2,1)}, bf16[1,512,2048]{2,1,0:T(8,128)(2,1)}, bf16[1,2048,512]{2,1,0:T(8,128)(2,1)}, f32[1,10]{1,0:T(1,128)}) custom-call(bf16[1,512,2048]{2,1,0:T(8,128)(2,1)S(1)} %get-tuple-element.11.gwg_ref, bf16[1,512,2048]{2,1,0:T(8,128)(2,1)S(1)} %get-tuple-element.12.gwu_ref, ...), custom_call_target="tpu_custom_call" | custom-call | tf_op jit(solution)/shard_map/finish/pallas_call | solution.py:509

commit v2 on v1

--- a/solution.py
+++ b/solution.py
@@ -11,6 +11,7 @@
 MESH = pl.DeviceIdType.MESH
 BF16 = jnp.bfloat16
 F32 = jnp.float32
+PIECES = 4
 
 
 def ceil_to(value, step):
@@ -179,39 +180,68 @@
         where = local_index(slots[e : e + 1], me_x * tok, (me_x + 1) * tok, rb)
         where_ref[e] = where
         picks.append((where == iota((rb, tok), 1)).astype(F32).astype(BF16))
-    loads[2].wait()
-    loads[3].wait()
-    for e in range(flight):
-        rows = [mm(picks[e], tokens[...], 1, 0), mm(picks[e], out_grad[...], 1, 0)]
-        pick_send[e] = jnp.concatenate(rows, axis=0).astype(BF16)
+    def pick_copy(i, k, peer, slot):
+        return remote(
+            pick_send.at[peer // GROUP, i],
+            pick_recv.at[slot, i],
+            pick_ssem.at[i, k],
+            pick_rsem.at[i, slot],
+            (me_d, peer),
+        )
+
+    for i, source in enumerate((tokens, out_grad)):
+        loads[2 + i].wait()
+        for e in range(flight):
+            rows = mm(picks[e], source[...], 1, 0)
+            if cfg.fold_pick:
+                rows = jnp.concatenate([rows[:, : fc // 2], rows[:, fc // 2 :]], axis=0)
+            pick_send[e, i] = pad_rows(rows, pick_send.shape[2]).astype(BF16)
+        if i == 0:
+            pl.semaphore_wait(barrier, len(x_peers) + len(d_peers))
+        for k, peer in enumerate(x_peers):
+            launch(pick_copy(i, k, peer, me_x))
     pick_recv[me_x] = pick_send[expert_here]
-    pl.semaphore_wait(barrier, len(x_peers) + len(d_peers))
-
-    def pick_copy(k, peer, slot):
-        return remote(
-            pick_send.at[peer // GROUP], pick_recv.at[slot], pick_ssem.at[k], pick_rsem.at[slot], (me_d, peer)
-        )
-
-    for k, peer in enumerate(x_peers):
-        launch(pick_copy(k, peer, me_x))
 
     slot_row = pick_row(slots.astype(F32), expert_here).astype(jnp.int32)
     gate_col = row_to_column(pick_row(gate_ref[...], expert_here))
-    place_x, place_g = [], []
-    empty = jnp.zeros((cap, rb), F32)
+    place_rows = [[], []]
+    empty = jnp.zeros((cap, pick_recv.shape[2] - rb), F32)
     for o in range(nx):
         mask = rank_mask(slot_row, o * tok, (o + 1) * tok, rb, 0).astype(F32)
-        place_x += [mask, empty]
-        place_g += [empty, mask]
-    place = jnp.concatenate(
-        [jnp.concatenate(place_x, axis=1), jnp.concatenate(place_g, axis=1)], axis=0
-    ).astype(BF16)
-    for k, peer in enumerate(x_peers):
-        pick_copy(k, peer, peer).wait_recv()
-    both = mm(place, pick_recv[...].reshape(nx * 2 * rb, fc), 1, 0)
-    x = both[:cap].astype(BF16)
-    scaled = (gate_col * both[cap:]).astype(BF16)
-    grads = both[cap:].astype(BF16)
+        place_rows[0] += [mask, empty]
+        place_rows[1] += [empty, mask]
+    place = [jnp.concatenate(blocks, axis=1) for blocks in place_rows[: 2 if cfg.fold_pick else 1]]
+    place = jnp.concatenate(place, axis=0).astype(BF16)
+
+    def placed(i):
+        for k, peer in enumerate(x_peers):
+            pick_copy(i, k, peer, peer).wait_recv()
+        rows = jnp.concatenate([pick_recv[o, i] for o in range(nx)], axis=0)
+        value = mm(place, rows, 1, 0)
+        if cfg.fold_pick:
+            value = jnp.concatenate([value[:cap], value[cap:]], axis=1)
+        return value
+
+    x = placed(0).astype(BF16)
+
+    fold_b = cfg.fold_b
+
+    def pack_b(value):
+        if fold_b:
+            value = jnp.concatenate([value[:, : width // 2], value[:, width // 2 :]], axis=0)
+        return pad_rows(value, cfg.rows_b).astype(BF16)
+
+    def unpack_b(block):
+        block = block.astype(F32)
+        if fold_b:
+            return jnp.concatenate([block[:cap], block[cap : 2 * cap]], axis=1)
+        return block[:cap]
+
+    def pack_a(value):
+        return pad_rows(value, cfg.rows_a).astype(BF16)
+
+    def unpack_a(block):
+        return block.astype(F32)[: 2 * cap]
 
     def first_pair(core):
         cols = pl.ds(pl.multiple_of(core * half, half), half)
@@ -240,7 +270,7 @@
             cols = slice(j * width, (j + 1) * width)
             total = own[:, cols] + got[:, cols]
             keep[j] = total
-            send[j] = pad_rows(total, send.shape[1]).astype(BF16)
+            send[j] = (pack_a, pack_b)[i](total)
         for k, peer in enumerate(z_peers):
             launch(z_copy(i, k, peer, my_z))
 
@@ -249,7 +279,7 @@
         total = (z_own_a, z_own_b)[i][my_z]
         for k, peer in enumerate(z_peers):
             z_copy(i, k, peer, peer).wait_recv()
-            total = total + recv[peer].astype(F32)[: total.shape[0]]
+            total = total + (unpack_a, unpack_b)[i](recv[peer])
         return total
 
     loads[4].wait()
@@ -257,6 +287,9 @@
     pair_send_a[...] = first_pair(other_c)
     launch(pair_copy(0))
     own_a = first_pair(my_c)
+    grads = placed(1)
+    scaled = (gate_col * grads).astype(BF16)
+    grads = grads.astype(BF16)
     z_start(0, own_a)
     loads[6].wait()
     pair_send_b[...] = hidden_part(other_c)
@@ -273,29 +306,26 @@
             launch(ag_copy(i, me_d, ag_ssem.at[i, k], peer * 2 + my_c))
         launch(ag_copy(i, me_d, fwd_ssem.at[i, 0], partner))
 
-    def ag_forward(i):
-        for k, peer in enumerate(z_peers):
-            owner = peer * 2 + my_c
-            ag_copy(i, owner, ag_ssem.at[i, k], owner).wait_recv()
-            launch(ag_copy(i, owner, fwd_ssem.at[i, k + 1], partner))
-
-    def ag_finish(i):
-        for k, peer in enumerate([my_z] + z_peers):
-            ag_copy(i, peer * 2 + other_c, fwd_ssem.at[i, k], partner).wait_recv()
+    def ag_forward(i, k):
+        owner = z_peers[k] * 2 + my_c
+        ag_copy(i, owner, ag_ssem.at[i, k], owner).wait_recv()
+        launch(ag_copy(i, owner, fwd_ssem.at[i, k + 1], partner))
+
+    def ag_finish(i, k):
+        owner = ([my_z] + z_peers)[k] * 2 + other_c
+        ag_copy(i, owner, fwd_ssem.at[i, k], partner).wait_recv()
 
     total = z_finish(0)
     pre_gate, pre_up = total[:cap], total[cap:]
     sig = 1.0 / (1.0 + jnp.exp(-pre_gate))
     silu = pre_gate * sig
     hidden = silu * pre_up
-    hid_blocks[me_d] = pad_rows(hidden, cfg.rows_b).astype(BF16)
+    hid_blocks[me_d] = pack_b(hidden)
     ag_start(0)
     gate_slope = pre_up * sig * (1.0 + pre_gate * (1.0 - sig))
     upstream = z_finish(1)
     grad_hidden = gate_col * upstream
-    side_blocks[me_d] = pad_rows(
-        jnp.concatenate([grad_hidden * gate_slope, grad_hidden * silu], axis=0), cfg.rows_a
-    ).astype(BF16)
+    side_blocks[me_d] = pack_a(jnp.concatenate([grad_hidden * gate_slope, grad_hidden * silu], axis=0))
     ag_start(1)
     gate_part = jnp.sum(hidden * upstream, axis=1, keepdims=True)
     lines = []
@@ -310,29 +340,66 @@
     for k, peer in enumerate(d_peers):
         launch(part_copy(k, peer, me_d))
 
-    ag_forward(0)
-
-    def gather(blocks, core, start):
-        parts = [blocks[j * 2 + core].astype(F32)[start : start + cap] for j in range(nz)]
-        return jnp.concatenate(parts, axis=1).astype(BF16)
-
-    def down_grad(core):
-        rows = pl.ds(pl.multiple_of(core * half, half), half)
-        gwd_ref[0, rows, :] = mm(gather(hid_blocks, core, 0), scaled, 0, 0).astype(BF16)
-
-    down_grad(my_c)
-    ag_forward(1)
-
-    def back_half(core):
-        cols = pl.ds(pl.multiple_of(core * half, half), half)
-        gate_side, up_side = gather(side_blocks, core, 0), gather(side_blocks, core, cap)
-        return gate_side, up_side, mm(gate_side, wg[:, cols], 1, 1) + mm(up_side, wu[:, cols], 1, 1)
-
-    mine = back_half(my_c)
-    ag_finish(0)
-    ag_finish(1)
-    others = back_half(other_c)
-    back = (mine[2] + others[2]).astype(BF16)
+    def unit_start(core, zs):
+        start = core * half
+        if len(zs) == 1:
+            start = start + zs[0] * width
+        size = len(zs) * width
+        return pl.ds(pl.multiple_of(start, size), size)
+
+    def unit_sides(core, zs):
+        blocks = [unpack_a(side_blocks[z * 2 + core]) for z in zs]
+        return [
+            jnp.concatenate([block[i * cap : (i + 1) * cap] for block in blocks], axis=1).astype(BF16)
+            for i in range(2)
+        ]
+
+    def unit_back(core, zs):
+        cols = unit_start(core, zs)
+        gate_side, up_side = unit_sides(core, zs)
+        return mm(gate_side, wg[:, cols], 1, 1) + mm(up_side, wu[:, cols], 1, 1)
+
+    def unit_grads(core, zs):
+        cols = unit_start(core, zs)
+        gate_side, up_side = unit_sides(core, zs)
+        hid = [unpack_b(hid_blocks[z * 2 + core]) for z in zs]
+        hid = jnp.concatenate(hid, axis=1).astype(BF16)
+        gwd_ref[0, cols, :] = mm(hid, scaled, 0, 0).astype(BF16)
+        gwg_ref[0, :, cols] = mm(x, gate_side, 0, 0).astype(BF16)
+        gwu_ref[0, :, cols] = mm(x, up_side, 0, 0).astype(BF16)
+
+    for k in range(nz - 1):
+        ag_forward(0, k)
+    if width % 128 == 0:
+        back = unit_back(my_c, [my_z])
+        unit_grads(my_c, [my_z])
+        ag_finish(0, 0)
+        ag_finish(1, 0)
+        back = back + unit_back(other_c, [my_z])
+        unit_grads(other_c, [my_z])
+        late = []
+        for k, peer in enumerate(z_peers):
+            ag_forward(1, k)
+            back = back + unit_back(my_c, [peer])
+            if k + 1 < len(z_peers):
+                unit_grads(my_c, [peer])
+            else:
+                late.append((my_c, [peer]))
+        for k, peer in enumerate(z_peers):
+            ag_finish(0, k + 1)
+            ag_finish(1, k + 1)
+            back = back + unit_back(other_c, [peer])
+            late.append((other_c, [peer]))
+    else:
+        for k in range(nz - 1):
+            ag_forward(1, k)
+        back = unit_back(my_c, list(range(nz)))
+        for k in range(nz):
+            ag_finish(0, k)
+            ag_finish(1, k)
+        back = back + unit_back(other_c, list(range(nz)))
+        late = [(my_c, list(range(nz))), (other_c, list(range(nz)))]
+    back = back.astype(BF16)
 
     for k, peer in enumerate(d_peers):
         part_copy(k, peer, peer).wait_recv()
@@ -356,11 +423,8 @@
     for k, peer in enumerate(x_peers):
         launch(back_copy(k, peer, me_x))
 
-    down_grad(other_c)
-    for core, (gate_side, up_side, _) in ((my_c, mine), (other_c, others)):
-        cols = pl.ds(pl.multiple_of(core * half, half), half)
-        gwg_ref[0, :, cols] = mm(x, gate_side, 0, 0).astype(BF16)
-        gwu_ref[0, :, cols] = mm(x, up_side, 0, 0).astype(BF16)
+    for core, zs in late:
+        unit_grads(core, zs)
     for k, peer in enumerate(x_peers):
         back_copy(k, peer, peer).wait_recv()
     for e in range(flight):
@@ -370,6 +434,11 @@
     )
     for copy in sends:
         copy.wait_send()
+
+
+def pieces(rows):
+    step = rows // PIECES
+    return [pl.ds(j * step, step) for j in range(PIECES)]
 
 
 def finish_kernel(
@@ -389,8 +458,9 @@
     sem,
 ):
     copies = [
-        pltpu.make_async_copy(src, dst, sem.at[i])
+        pltpu.make_async_copy(src.at[:, rows], dst.at[:, rows], sem.at[i, j])
         for i, (src, dst) in enumerate(((gwg_ref, wg_out), (gwu_ref, wu_out), (gwd_ref, wd_out)))
+        for j, rows in enumerate(pieces(src.shape[1]))
     ]
     for copy in copies:
         copy.start()
@@ -401,8 +471,8 @@
         term = mm(spread, ret_ref[e].astype(BF16), 0, 0)
         total = term if total is None else total + term
     tok_vmem[...] = total.astype(BF16)
-    copies.append(pltpu.make_async_copy(tok_vmem, tok_out, sem.at[3]))
-    copies[3].start()
+    copies.append(pltpu.make_async_copy(tok_vmem, tok_out, sem.at[3, 0]))
+    copies[-1].start()
     wide = cfg.cap // GROUP
     first = lax.rem(me_x, GROUP) * wide
     gates = jnp.zeros((1, wide), F32)
@@ -435,7 +505,10 @@
     c.rb = ceil_to(most, 8)
     c.gate_rows = ceil_to(c.cap, c.width) // c.width
     c.part_rows = ceil_to(c.gate_rows, 8)
-    c.rows_a, c.rows_b = ceil_to(2 * c.cap, 16), ceil_to(c.cap, 16)
+    c.fold_b, c.fold_pick = c.width % 256 == 0, c.fc % 256 == 0
+    c.rows_a = ceil_to(2 * c.cap, 16)
+    c.rows_b, cols_b = (c.rows_a, c.width // 2) if c.fold_b else (ceil_to(c.cap, 16), c.width)
+    pick = (ceil_to(2 * c.rb, 16), c.fc // 2) if c.fold_pick else (ceil_to(c.rb, 16), c.fc)
     c.back_rows = ceil_to(c.rb + 2 * c.gate_rows, 16)
     vmem = pl.BlockSpec(memory_space=pltpu.VMEM)
     hbm = pl.BlockSpec(memory_space=pltpu.HBM)
@@ -468,8 +541,8 @@
             pltpu.VMEM((c.fc, ffq), BF16),
             pltpu.VMEM((c.fc, ffq), BF16),
             pltpu.VMEM((ffq, c.fc), BF16),
-            pltpu.VMEM((c.flight, 2 * c.rb, c.fc), BF16),
-            pltpu.VMEM((c.nx, 2 * c.rb, c.fc), BF16),
+            pltpu.VMEM((c.flight, 2) + pick, BF16),
+            pltpu.VMEM((c.nx, 2) + pick, BF16),
             pltpu.VMEM((2 * c.cap, c.half), F32),
             pltpu.VMEM((c.cap, c.half), F32),
             pltpu.VMEM((2 * c.cap, c.half), F32),
@@ -477,17 +550,17 @@
             pltpu.VMEM((c.nz, 2 * c.cap, c.width), F32),
             pltpu.VMEM((c.nz, c.cap, c.width), F32),
             pltpu.VMEM((c.nz, c.rows_a, c.width), BF16),
-            pltpu.VMEM((c.nz, c.rows_b, c.width), BF16),
+            pltpu.VMEM((c.nz, c.rows_b, cols_b), BF16),
             pltpu.VMEM((c.nz, c.rows_a, c.width), BF16),
-            pltpu.VMEM((c.nz, c.rows_b, c.width), BF16),
-            pltpu.VMEM((nd, c.rows_b, c.width), BF16),
+            pltpu.VMEM((c.nz, c.rows_b, cols_b), BF16),
+            pltpu.VMEM((nd, c.rows_b, cols_b), BF16),
             pltpu.VMEM((nd, c.rows_a, c.width), BF16),
             pltpu.VMEM((nd, c.part_rows, c.width), F32),
             pltpu.VMEM((c.nx, c.back_rows, c.fc), BF16),
             pltpu.VMEM((c.nx, c.back_rows, c.fc), BF16),
             dma((7,)),
-            dma((c.nx,)),
-            dma((c.nx,)),
+            dma((2, c.nx)),
+            dma((2, c.nx)),
             dma((2,)),
             dma((2,)),
             dma((2, c.nz)),
@@ -511,7 +584,7 @@
         out_shape=(shape((c.tok, c.fc), BF16),) + grads + (shape((1, c.cap // GROUP), F32),),
         in_specs=[vmem] * 6,
         out_specs=[hbm] * 4 + [vmem],
-        scratch_shapes=[pltpu.VMEM((c.tok, c.fc), BF16), dma((4,))],
+        scratch_shapes=[pltpu.VMEM((c.tok, c.fc), BF16), dma((4, PIECES))],
         compiler_params=pltpu.CompilerParams(vmem_limit_bytes=40 * 1024 * 1024),
         name="finish",
     )(*parts)

time: 34.9 us -> 34.7 us (level)
  no operation moved by 1% of the time
where the time goes in v2:
time: 34.7 us; the launch traced here: 34.5 us
  Pallas kernels  33.9 us (98%)
  between operations  0.64 us (2%)
    pallas_call x1, Pallas kernels, per_device(): pl.pallas_call(functools.partial(exchange_kernel, c), out_shape=grads + (...  30.5 us
    pallas_call x1, Pallas kernels, per_device(): pl.pallas_call(functools.partial(finish_kernel, c), out_shape=(shape((c.t...  3.39 us

profile of v2, /device:TPU:0, one launch (start us, length us, event | category | flops | bytes accessed | tf_op | source)
XLA Modules:
  0.0 34.5 jit_solution(7068441204170052956)
XLA Ops:
  0.6 30.5 %exchange.1 = (bf16[1,512,2048]{2,1,0:T(8,128)(2,1)S(1)}, bf16[1,512,2048]{2,1,0:T(8,128)(2,1)S(1)}, bf16[1,2048,512]{2,1,0:T(8,128)(2,1)S(1)}, f32[1,24,512]{2,...) custom-call(s32[1,40]{1,0:T(1,128)} %slot_hbm.1, f32[1,40]{1,0:T(1,128)} %gate_hbm.1, ...), custom_call_target="tpu_custom_call" | custom-call | tf_op jit(solution)/shard_map/exchange/pallas_call | solution.py:526
  31.1 3.4 %finish.1 = (bf16[320,512]{1,0:T(8,128)(2,1)}, bf16[1,512,2048]{2,1,0:T(8,128)(2,1)}, bf16[1,512,2048]{2,1,0:T(8,128)(2,1)}, bf16[1,2048,512]{2,1,0:T(8,128)(2,1)}, f32[1,10]{1,0:T(1,128)}) custom-call(bf16[1,512,2048]{2,1,0:T(8,128)(2,1)S(1)} %get-tuple-element.11.gwg_ref, bf16[1,512,2048]{2,1,0:T(8,128)(2,1)S(1)} %get-tuple-element.12.gwu_ref, ...), custom_call_target="tpu_custom_call" | custom-call | tf_op jit(solution)/shard_map/finish/pallas_call | solution.py:582

commit v3 on v2

--- a/solution.py
+++ b/solution.py
@@ -68,6 +68,13 @@
     if value.shape[0] == rows:
         return value
     return jnp.concatenate([value, jnp.zeros((rows - value.shape[0], value.shape[1]), value.dtype)], axis=0)
+
+
+def across(place, offset, bits):
+    for bit in bits:
+        if offset & bit:
+            place = place + bit * (1 - 2 * lax.rem(place // bit, 2))
+    return place
 
 
 def exchange_kernel(
@@ -301,18 +308,28 @@
         block = (hid_blocks, side_blocks)[i].at[owner]
         return remote(block, block, send_sem, ag_rsem.at[i, owner], (target, me_x))
 
+    bits = [2**k for k in range(nz.bit_length() - 1)]
+    offsets = sorted(range(1, nz), key=lambda o: (bin(o).count("1"), -o))
+    chips = [across(my_z, o, bits) for o in offsets]
+
+    def ag_spread(i, offset, slot):
+        owner = across(my_z, offset, bits) * 2 + my_c
+        for k, bit in enumerate(bits):
+            if offset == 0 or bit < (offset & -offset):
+                launch(ag_copy(i, owner, ag_ssem.at[i, slot, k], across(my_z, bit, bits) * 2 + my_c))
+        launch(ag_copy(i, owner, fwd_ssem.at[i, slot], partner))
+
     def ag_start(i):
-        for k, peer in enumerate(z_peers):
-            launch(ag_copy(i, me_d, ag_ssem.at[i, k], peer * 2 + my_c))
-        launch(ag_copy(i, me_d, fwd_ssem.at[i, 0], partner))
+        ag_spread(i, 0, 0)
 
     def ag_forward(i, k):
-        owner = z_peers[k] * 2 + my_c
-        ag_copy(i, owner, ag_ssem.at[i, k], owner).wait_recv()
-        launch(ag_copy(i, owner, fwd_ssem.at[i, k + 1], partner))
+        low = offsets[k] & -offsets[k]
+        source = across(my_z, low, bits) * 2 + my_c
+        ag_copy(i, chips[k] * 2 + my_c, ag_ssem.at[i, 0, 0], source).wait_recv()
+        ag_spread(i, offsets[k], k + 1)
 
     def ag_finish(i, k):
-        owner = ([my_z] + z_peers)[k] * 2 + other_c
+        owner = ([my_z] + chips)[k] * 2 + other_c
         ag_copy(i, owner, fwd_ssem.at[i, k], partner).wait_recv()
 
     total = z_finish(0)
@@ -378,14 +395,14 @@
         back = back + unit_back(other_c, [my_z])
         unit_grads(other_c, [my_z])
         late = []
-        for k, peer in enumerate(z_peers):
+        for k, peer in enumerate(chips):
             ag_forward(1, k)
             back = back + unit_back(my_c, [peer])
-            if k + 1 < len(z_peers):
+            if k + 1 < len(chips):
                 unit_grads(my_c, [peer])
             else:
                 late.append((my_c, [peer]))
-        for k, peer in enumerate(z_peers):
+        for k, peer in enumerate(chips):
             ag_finish(0, k + 1)
             ag_finish(1, k + 1)
             back = back + unit_back(other_c, [peer])
@@ -565,7 +582,7 @@
             dma((2,)),
             dma((2, c.nz)),
             dma((2, c.nz)),
-            dma((2, c.nz)),
+            dma((2, c.nz, c.nz.bit_length())),
             dma((2, c.nz)),
             dma((2, nd)),
             dma((nd,)),

time: 34.7 us -> 37.4 us (1.078)
  Pallas kernels: 33.9 us -> 36.6 us
    pallas_call x1, Pallas kernels: 30.5 us -> 33.2 us  [per_device(): pl.pallas_call(functools.partial(exchange_kernel, c), out_shape=grads + (...]
where the time goes in v3:
time: 37.4 us; the launch traced here: 37.2 us
  Pallas kernels  36.6 us (98%)
  between operations  0.64 us (2%)
    pallas_call x1, Pallas kernels, per_device(): pl.pallas_call(functools.partial(exchange_kernel, c), out_shape=grads + (...  33.2 us
    pallas_call x1, Pallas kernels, per_device(): pl.pallas_call(functools.partial(finish_kernel, c), out_shape=(shape((c.t...  3.39 us

profile of v3, /device:TPU:0, one launch (start us, length us, event | category | flops | bytes accessed | tf_op | source)
XLA Modules:
  0.0 37.2 jit_solution(10521238377906260532)
XLA Ops:
  0.6 33.2 %exchange.1 = (bf16[1,512,2048]{2,1,0:T(8,128)(2,1)S(1)}, bf16[1,512,2048]{2,1,0:T(8,128)(2,1)S(1)}, bf16[1,2048,512]{2,1,0:T(8,128)(2,1)S(1)}, f32[1,24,512]{2,...) custom-call(s32[1,40]{1,0:T(1,128)} %slot_hbm.1, f32[1,40]{1,0:T(1,128)} %gate_hbm.1, ...), custom_call_target="tpu_custom_call" | custom-call | tf_op jit(solution)/shard_map/exchange/pallas_call | solution.py:543
  33.8 3.4 %finish.1 = (bf16[320,512]{1,0:T(8,128)(2,1)}, bf16[1,512,2048]{2,1,0:T(8,128)(2,1)}, bf16[1,512,2048]{2,1,0:T(8,128)(2,1)}, bf16[1,2048,512]{2,1,0:T(8,128)(2,1)}, f32[1,10]{1,0:T(1,128)}) custom-call(bf16[1,512,2048]{2,1,0:T(8,128)(2,1)S(1)} %get-tuple-element.11.gwg_ref, bf16[1,512,2048]{2,1,0:T(8,128)(2,1)S(1)} %get-tuple-element.12.gwu_ref, ...), custom_call_target="tpu_custom_call" | custom-call | tf_op jit(solution)/shard_map/finish/pallas_call | solution.py:599
